TPU v7x, 512 devices: a whole 4x4x16 slice. The times are simulated.
512 devices in a mesh: seq: 32 (over x, y, core), key: 16 (over z).
Axes of the slice: x: 4, y: 4, z: 16, core: 2. Of those that a mesh axis runs over, the one named last changes fastest.
Arguments:
- query_rows: bfloat16 [8192, 16, 256], P('seq', None, 'key'), may hold values from -0.375 to 0.375
- key_rows: bfloat16 [8192, 16, 256], P('seq', None, 'key'), may hold values from -0.1875 to 0.1875
- value_rows: bfloat16 [8192, 16, 256], P('seq', 'key'), may hold values from -6 to 6
- out_grad: bfloat16 [8192, 16, 256], P('seq', 'key')
- log_gates: float32 [16, 8192], P('key', 'seq'), may hold values from -0.8 to 0, as said below
- write_rate: float32 [16, 8192], P('key', 'seq'), may hold values from 0.1 to 0.8
- group_inverse: bfloat16 [64, 16, 128, 128], P('seq', 'key'), as said below
- states: bfloat16 [64, 16, 256, 256], P('seq', None, 'key'), may hold values from -0.75 to 0.75
Outputs:
- grad_query: bfloat16 [8192, 16, 256], P('seq', None, 'key')
- grad_key: bfloat16 [8192, 16, 256], P('seq', None, 'key')
- grad_value: bfloat16 [8192, 16, 256], P('seq', 'key')
- grad_square: float32 [], replicated
Inputs may be any that keep to these rules, and one draw needn't show every extreme that they name: `group_inverse`: each group's matrix is unit lower triangular: ones on the diagonal, zeros above it. `log_gates`: every entry is the logarithm of a decay factor, never positive.
All inputs are finite; a program needn't handle non-finite values.
Results may differ from a plain program's by a relative error of at most 0.007.
Values may be sent and summed in bfloat16 or wider, within the bound.
No kernel may reach another device: no remote copies, remote signals or barrier semaphores. Data moves between devices by JAX's collectives and lax.ppermute only.
A program may use at most 128 MiB of HBM per device.

v0:
```python
import jax
import jax.numpy as jnp
from jax import lax
from jax.sharding import PartitionSpec as P

highest_mode = lax.Precision.HIGHEST


def from_behind(value, axis, steps):
    count = lax.axis_size(axis)
    first, last = (max(0, -steps), min(count, count - steps))
    return lax.ppermute(value, axis, [(source, source + steps) for source in range(first, last)])


def mixed_dot(form, left, right):
    return jnp.einsum(form, left, right, preferred_element_type=jnp.float32)


def precise_product(form, left, right):
    return jnp.einsum(form, left.astype(jnp.float32), right, precision=highest_mode)


def linear_part(state_in, write_block, key_block, decay_block):
    through = precise_product("thk,hkm->thm", key_block, state_in)
    return decay_block[:, None, None] * state_in - precise_product(
        "thk,thm->hkm", write_block, through
    )


def device_map(state_out, written_keys, key_result, end_decay, offset_term):

    def group_step(state_in, pieces):
        write_block, key_block, decay_block, offset_block = pieces
        return (linear_part(state_in, write_block, key_block, decay_block) + offset_block, state_in)

    return lax.scan(
        group_step, state_out, (written_keys, key_result, end_decay, offset_term), reverse=True
    )


def token_wise(factor):
    return jnp.transpose(factor, (0, 2, 1))[:, :, :, None]


def square_sum(array):
    return jnp.sum(jnp.square(array.astype(jnp.float32)))


def local(query_rows, key_rows, value_rows, out_grad, log_gates, write_rate, group_inverse, states):
    halfway_point = jnp.bfloat16
    query_heads, key_heads, state_heads = (
        lax.all_to_all(query_rows, "key", split_axis=1, concat_axis=2, tiled=True),
        lax.all_to_all(key_rows, "key", split_axis=1, concat_axis=2, tiled=True),
        lax.all_to_all(states, "key", split_axis=1, concat_axis=2, tiled=True),
    )
    group_count, head_local, group_len, _ = group_inverse.shape
    token_count, _, key_width = query_heads.shape
    value_width = value_rows.shape[2]
    query_blk = query_heads.reshape(group_count, group_len, head_local, key_width)
    key_blk = key_heads.reshape(group_count, group_len, head_local, key_width)
    value_blk = value_rows.reshape(group_count, group_len, head_local, value_width)
    grad_blk = out_grad.reshape(group_count, group_len, head_local, value_width)
    gate_blk = jnp.transpose(log_gates.reshape(head_local, group_count, group_len), (1, 0, 2))
    rate_blk = jnp.transpose(write_rate.reshape(head_local, group_count, group_len), (1, 0, 2))
    gamma = jnp.cumsum(gate_blk, axis=2)
    final_gamma_value = gamma[:, :, -1:]
    incoming_decay = jnp.exp(gamma)
    outgoing_decay = jnp.exp(final_gamma_value - gamma)
    row_ids = lax.broadcasted_iota(jnp.int32, (group_len, group_len), 0)
    col_ids = lax.broadcasted_iota(jnp.int32, (group_len, group_len), 1)
    lower = row_ids >= col_ids
    spread = gamma[:, :, :, None] - gamma[:, :, None, :]
    decay_mask = jnp.where(lower, jnp.exp(jnp.where(lower, spread, 0.0)), 0.0)
    key_scaled = (key_blk * token_wise(rate_blk * incoming_decay)).astype(halfway_point)
    written_keys = mixed_dot("nhts,nshk->nthk", group_inverse, key_scaled).astype(halfway_point)
    scaled_values = (value_blk * token_wise(rate_blk)).astype(halfway_point)
    fresh_values = (
        mixed_dot("nhts,nshv->nthv", group_inverse, scaled_values)
        - mixed_dot("nthk,nhkv->nthv", written_keys, state_heads)
    ).astype(halfway_point)
    score_mat = (mixed_dot("nthk,nshk->nhts", query_blk, key_blk) * decay_mask).astype(
        halfway_point
    )
    key_result = (key_blk * token_wise(outgoing_decay)).astype(halfway_point)
    incoming_query = (query_blk * token_wise(incoming_decay)).astype(halfway_point)
    inner_gradient = mixed_dot("nhts,nthv->nshv", score_mat, grad_blk)
    offset_term = mixed_dot("nthk,nthv->nhkv", incoming_query, grad_blk) - precise_product(
        "nthk,nthv->nhkv", written_keys, inner_gradient
    )
    end_decay = jnp.exp(final_gamma_value[:, :, 0])
    empty_state = jnp.zeros((head_local, key_width, value_width), jnp.float32)

    def relay_hop(hop_index, incoming):
        state_in, _ = device_map(incoming, written_keys, key_result, end_decay, offset_term)
        return from_behind(state_in, "seq", -1)

    state_out = lax.fori_loop(0, lax.axis_size("seq") - 1, relay_hop, empty_state)
    _, state_gradient = device_map(state_out, written_keys, key_result, end_decay, offset_term)
    value_rounding = (
        inner_gradient + precise_product("nthk,nhkv->nthv", key_result, state_gradient)
    ).astype(halfway_point)
    value_grad_blk = (
        token_wise(rate_blk) * mixed_dot("nhts,nthv->nshv", group_inverse, value_rounding)
    ).astype(halfway_point)
    score_gradient = (mixed_dot("nthv,nshv->nhts", grad_blk, fresh_values) * decay_mask).astype(
        halfway_point
    )
    write_gradient = (-mixed_dot("nthv,nhkv->nthk", value_rounding, state_heads)).astype(
        halfway_point
    )
    state_rounding = state_gradient.astype(halfway_point)
    query_grad_blk = (
        token_wise(incoming_decay) * mixed_dot("nthv,nhkv->nthk", grad_blk, state_heads)
        + mixed_dot("nhts,nshk->nthk", score_gradient, key_blk)
    ).astype(halfway_point)
    key_grad_blk = (
        mixed_dot("nhts,nthk->nshk", score_gradient, query_blk)
        + token_wise(outgoing_decay) * mixed_dot("nthv,nhkv->nthk", fresh_values, state_rounding)
        + token_wise(rate_blk * incoming_decay)
        * mixed_dot("nhts,nthk->nshk", group_inverse, write_gradient)
    ).astype(halfway_point)
    query_grad_heads = query_grad_blk.reshape(token_count, head_local, key_width)
    key_grad_heads = key_grad_blk.reshape(token_count, head_local, key_width)
    grad_value = value_grad_blk.reshape(token_count, head_local, value_width)
    grad_query, grad_key = (
        lax.all_to_all(query_grad_heads, "key", split_axis=2, concat_axis=1, tiled=True),
        lax.all_to_all(key_grad_heads, "key", split_axis=2, concat_axis=1, tiled=True),
    )
    value_square = square_sum(grad_value)
    partial_value = square_sum(grad_query) + square_sum(grad_key) + value_square
    summed = lax.psum(partial_value, ("seq", "key"))
    entries = (
        token_count * lax.axis_size("seq") * query_rows.shape[1] * (2 * key_width + value_width)
    )
    return (grad_query, grad_key, grad_value, summed / entries)


def solution(mesh):
    in_specs = (
        P("seq", None, "key"),
        P("seq", None, "key"),
        P("seq", "key", None),
        P("seq", "key", None),
        P("key", "seq"),
        P("key", "seq"),
        P("seq", "key", None, None),
        P("seq", None, "key", None),
    )
    out_specs = (P("seq", None, "key"), P("seq", None, "key"), P("seq", "key", None), P())
    return jax.shard_map(local, mesh=mesh, in_specs=in_specs, out_specs=out_specs, check_vma=False)
```

profile of v0, /device:TPU:1, one launch (start us, length us, event | category | flops | bytes accessed | tf_op | source)
XLA Modules:
  0.0 631.2 jit_solution(10819537718962490288)
XLA Ops:
  0.7 15.9 %all-to-all-start.1 = ((bf16[256,16,16]{0,2,1:T(8,128)(2,1)}), bf16[256,16,16]{0,2,1:T(8,128)(2,1)S(1)}, u32[]{:S(2)}, u32[]{:S(2)}) async-start(bf16[256,16,16]{0,2,1:T(8,128)(2,1)} %param.15), calls=%async_computation.1 | async-start | bytes 262144 | tf_op jit(solution)/shard_map/all_to_all | solution.py:53
  17.9 10.7 %all-to-all-done.1 = bf16[256,16,16]{0,2,1:T(8,128)(2,1)S(1)} async-done(((bf16[256,16,16]{0,2,1:T(8,128)(2,1)}), bf16[256,16,16]{0,2,1:T(8,128)(2,1)S(1)}, u32[]{:S(2)}, u32[]{:S(2)}) %all-to-all-start.1) | async-done | bytes 131104 | tf_op jit(solution)/shard_map/all_to_all | solution.py:53
  36.8 9.7 %all-to-all-done.3 = bf16[256,16,16]{0,2,1:T(8,128)(2,1)S(1)} async-done(((bf16[256,16,16]{0,2,1:T(8,128)(2,1)}), bf16[256,16,16]{0,2,1:T(8,128)(2,1)S(1)}, u32[]{:S(2)}, u32[]{:S(2)}) %all-to-all-start.3) | async-done | bytes 131104 | tf_op jit(solution)/shard_map/all_to_all | solution.py:52
  54.0 393.7 %while.57 = (s32[]{:T(128)}, f32[1,256,256]{2,1,0:T(8,128)S(1)}, f32[2,1]{0,1:T(1,128)S(1)}, bf16[2,128,1,256]{3,1,2,0:T(8,128)(2,1)S(1)}, bf16[2,128,1,256]{3,1...) while((s32[]{:T(128)}, f32[1,256,256]{2,1,0:T(8,128)S(1)}, ...), condition=%wide.region_4.5_spmd, body=%wide.region_1.4_spmd.sunk | while | flops 201523200 | bytes 3015986 | solution.py:97
  222.6 7.9 %collective-permute-done = f32[1,256,256]{2,1,0:T(8,128)S(1)} collective-permute-done((f32[1,256,256]{2,1,0:T(8,128)S(1)}, f32[1,256,256]{2,1,0:T(8,128)S(1)}, u32[]{:S(2)}, u32[]{:S(2)}) %collective-permute-start) | collective-permute-done | bytes 262176 | tf_op jit(solution)/shard_map/while/body/eval_jaxpr/ppermute | solution.py:12
  236.2 7.9 %collective-permute-done = f32[1,256,256]{2,1,0:T(8,128)S(1)} collective-permute-done((f32[1,256,256]{2,1,0:T(8,128)S(1)}, f32[1,256,256]{2,1,0:T(8,128)S(1)}, u32[]{:S(2)}, u32[]{:S(2)}) %collective-permute-start) | collective-permute-done | bytes 262176 | tf_op jit(solution)/shard_map/while/body/eval_jaxpr/ppermute | solution.py:12
  249.8 7.9 %collective-permute-done = f32[1,256,256]{2,1,0:T(8,128)S(1)} collective-permute-done((f32[1,256,256]{2,1,0:T(8,128)S(1)}, f32[1,256,256]{2,1,0:T(8,128)S(1)}, u32[]{:S(2)}, u32[]{:S(2)}) %collective-permute-start) | collective-permute-done | bytes 262176 | tf_op jit(solution)/shard_map/while/body/eval_jaxpr/ppermute | solution.py:12
  263.4 7.9 %collective-permute-done = f32[1,256,256]{2,1,0:T(8,128)S(1)} collective-permute-done((f32[1,256,256]{2,1,0:T(8,128)S(1)}, f32[1,256,256]{2,1,0:T(8,128)S(1)}, u32[]{:S(2)}, u32[]{:S(2)}) %collective-permute-start) | collective-permute-done | bytes 262176 | tf_op jit(solution)/shard_map/while/body/eval_jaxpr/ppermute | solution.py:12
  276.9 7.9 %collective-permute-done = f32[1,256,256]{2,1,0:T(8,128)S(1)} collective-permute-done((f32[1,256,256]{2,1,0:T(8,128)S(1)}, f32[1,256,256]{2,1,0:T(8,128)S(1)}, u32[]{:S(2)}, u32[]{:S(2)}) %collective-permute-start) | collective-permute-done | bytes 262176 | tf_op jit(solution)/shard_map/while/body/eval_jaxpr/ppermute | solution.py:12
  290.5 7.9 %collective-permute-done = f32[1,256,256]{2,1,0:T(8,128)S(1)} collective-permute-done((f32[1,256,256]{2,1,0:T(8,128)S(1)}, f32[1,256,256]{2,1,0:T(8,128)S(1)}, u32[]{:S(2)}, u32[]{:S(2)}) %collective-permute-start) | collective-permute-done | bytes 262176 | tf_op jit(solution)/shard_map/while/body/eval_jaxpr/ppermute | solution.py:12
  304.1 7.9 %collective-permute-done = f32[1,256,256]{2,1,0:T(8,128)S(1)} collective-permute-done((f32[1,256,256]{2,1,0:T(8,128)S(1)}, f32[1,256,256]{2,1,0:T(8,128)S(1)}, u32[]{:S(2)}, u32[]{:S(2)}) %collective-permute-start) | collective-permute-done | bytes 262176 | tf_op jit(solution)/shard_map/while/body/eval_jaxpr/ppermute | solution.py:12
  317.7 7.9 %collective-permute-done = f32[1,256,256]{2,1,0:T(8,128)S(1)} collective-permute-done((f32[1,256,256]{2,1,0:T(8,128)S(1)}, f32[1,256,256]{2,1,0:T(8,128)S(1)}, u32[]{:S(2)}, u32[]{:S(2)}) %collective-permute-start) | collective-permute-done | bytes 262176 | tf_op jit(solution)/shard_map/while/body/eval_jaxpr/ppermute | solution.py:12
  331.2 7.9 %collective-permute-done = f32[1,256,256]{2,1,0:T(8,128)S(1)} collective-permute-done((f32[1,256,256]{2,1,0:T(8,128)S(1)}, f32[1,256,256]{2,1,0:T(8,128)S(1)}, u32[]{:S(2)}, u32[]{:S(2)}) %collective-permute-start) | collective-permute-done | bytes 262176 | tf_op jit(solution)/shard_map/while/body/eval_jaxpr/ppermute | solution.py:12
  344.8 7.9 %collective-permute-done = f32[1,256,256]{2,1,0:T(8,128)S(1)} collective-permute-done((f32[1,256,256]{2,1,0:T(8,128)S(1)}, f32[1,256,256]{2,1,0:T(8,128)S(1)}, u32[]{:S(2)}, u32[]{:S(2)}) %collective-permute-start) | collective-permute-done | bytes 262176 | tf_op jit(solution)/shard_map/while/body/eval_jaxpr/ppermute | solution.py:12
  358.4 7.9 %collective-permute-done = f32[1,256,256]{2,1,0:T(8,128)S(1)} collective-permute-done((f32[1,256,256]{2,1,0:T(8,128)S(1)}, f32[1,256,256]{2,1,0:T(8,128)S(1)}, u32[]{:S(2)}, u32[]{:S(2)}) %collective-permute-start) | collective-permute-done | bytes 262176 | tf_op jit(solution)/shard_map/while/body/eval_jaxpr/ppermute | solution.py:12
  372.0 7.9 %collective-permute-done = f32[1,256,256]{2,1,0:T(8,128)S(1)} collective-permute-done((f32[1,256,256]{2,1,0:T(8,128)S(1)}, f32[1,256,256]{2,1,0:T(8,128)S(1)}, u32[]{:S(2)}, u32[]{:S(2)}) %collective-permute-start) | collective-permute-done | bytes 262176 | tf_op jit(solution)/shard_map/while/body/eval_jaxpr/ppermute | solution.py:12
  385.5 7.9 %collective-permute-done = f32[1,256,256]{2,1,0:T(8,128)S(1)} collective-permute-done((f32[1,256,256]{2,1,0:T(8,128)S(1)}, f32[1,256,256]{2,1,0:T(8,128)S(1)}, u32[]{:S(2)}, u32[]{:S(2)}) %collective-permute-start) | collective-permute-done | bytes 262176 | tf_op jit(solution)/shard_map/while/body/eval_jaxpr/ppermute | solution.py:12
  412.7 7.9 %collective-permute-done = f32[1,256,256]{2,1,0:T(8,128)S(1)} collective-permute-done((f32[1,256,256]{2,1,0:T(8,128)S(1)}, f32[1,256,256]{2,1,0:T(8,128)S(1)}, u32[]{:S(2)}, u32[]{:S(2)}) %collective-permute-start) | collective-permute-done | bytes 262176 | tf_op jit(solution)/shard_map/while/body/eval_jaxpr/ppermute | solution.py:12
  426.2 7.9 %collective-permute-done = f32[1,256,256]{2,1,0:T(8,128)S(1)} collective-permute-done((f32[1,256,256]{2,1,0:T(8,128)S(1)}, f32[1,256,256]{2,1,0:T(8,128)S(1)}, u32[]{:S(2)}, u32[]{:S(2)}) %collective-permute-start) | collective-permute-done | bytes 262176 | tf_op jit(solution)/shard_map/while/body/eval_jaxpr/ppermute | solution.py:12
  439.8 7.9 %collective-permute-done = f32[1,256,256]{2,1,0:T(8,128)S(1)} collective-permute-done((f32[1,256,256]{2,1,0:T(8,128)S(1)}, f32[1,256,256]{2,1,0:T(8,128)S(1)}, u32[]{:S(2)}, u32[]{:S(2)}) %collective-permute-start) | collective-permute-done | bytes 262176 | tf_op jit(solution)/shard_map/while/body/eval_jaxpr/ppermute | solution.py:12
  456.1 11.2 %all-to-all-start.4 = ((bf16[16,2,2048]{2,1,0:T(2,128)(2,1)}), bf16[16,2,2048]{2,1,0:T(2,128)(2,1)S(1)}, u32[]{:S(2)}, u32[]{:S(2)}) async-start(bf16[16,2,2048]{2,1,0:T(2,128)(2,1)} %reshape.369), calls=%async_computation.4 | async-start | bytes 262144 | tf_op jit(solution)/shard_map/all_to_all | solution.py:127
  470.0 9.2 %all-to-all-done.4 = bf16[16,2,2048]{2,1,0:T(2,128)(2,1)S(1)} async-done(((bf16[16,2,2048]{2,1,0:T(2,128)(2,1)}), bf16[16,2,2048]{2,1,0:T(2,128)(2,1)S(1)}, u32[]{:S(2)}, u32[]{:S(2)}) %all-to-all-start.4) | async-done | bytes 131104 | tf_op jit(solution)/shard_map/all_to_all | solution.py:127
  484.6 10.4 %all-to-all-done.2 = bf16[16,2,2048]{2,1,0:T(2,128)(2,1)S(1)} async-done(((bf16[16,2,2048]{2,1,0:T(2,128)(2,1)}), bf16[16,2,2048]{2,1,0:T(2,128)(2,1)S(1)}, u32[]{:S(2)}, u32[]{:S(2)}) %all-to-all-start.2) | async-done | bytes 131104 | tf_op jit(solution)/shard_map/all_to_all | solution.py:126
  498.3 129.8 %psum.7 = f32[]{:T(128)} all-reduce(f32[]{:T(128)S(6)} %add.89), channel_id=1, replica_groups=mesh['seq'=32,'key'=16] {'seq','key'}, use_global_device_ids=true, to_apply=%region_10.11 | all-reduce | flops 1 | bytes 8 | tf_op jit(solution)/shard_map/psum | solution.py:131
  (363 shorter events, 420.2 us)
Async XLA Ops:
  0.7 27.9 %all-to-all-start.1 = ((bf16[256,16,16]{0,2,1:T(8,128)(2,1)}), bf16[256,16,16]{0,2,1:T(8,128)(2,1)S(1)}, u32[]{:S(2)}, u32[]{:S(2)}) async-start(bf16[256,16,16]{0,2,1:T(8,128)(2,1)} %param.15), calls=%async_computation.1 | async-start | bytes 262144 | tf_op jit(solution)/shard_map/all_to_all | solution.py:53
  28.6 17.9 %all-to-all-start.3 = ((bf16[256,16,16]{0,2,1:T(8,128)(2,1)}), bf16[256,16,16]{0,2,1:T(8,128)(2,1)S(1)}, u32[]{:S(2)}, u32[]{:S(2)}) async-start(bf16[256,16,16]{0,2,1:T(8,128)(2,1)} %param.14), calls=%async_computation.3 | async-start | bytes 262144 | tf_op jit(solution)/shard_map/all_to_all | solution.py:52
  46.5 405.4 %all-to-all-start = ((bf16[2,16,16,256]{3,2,0,1:T(8,128)(2,1)}), bf16[2,16,16,256]{3,2,0,1:T(8,128)(2,1)S(1)}, u32[]{:S(2)}, u32[]{:S(2)}) async-start(bf16[2,16,16,256]{3,2,0,1:T(8,128)(2,1)} %copy.117), calls=%async_computation | async-start | bytes 524288 | tf_op jit(solution)/shard_map/all_to_all | solution.py:54
  57.7 9.4 %collective-permute-start = (f32[1,256,256]{2,1,0:T(8,128)S(1)}, f32[1,256,256]{2,1,0:T(8,128)S(1)}, u32[]{:S(2)}, u32[]{:S(2)}) collective-permute-start(f32[1,256,256]{2,1,0:T(8,128)S(1)} %get-tuple-element.637), channel_id=1, source_target_pairs={{16,0},{32,16},{48,32},{64,48},{80,64},{96,80},{112,96},{128,112},... | collective-permute-start | bytes 786440 | tf_op jit(solution)/shard_map/while/body/eval_jaxpr/ppermute | solution.py:12
  208.5 8.4 %collective-permute-start = (f32[1,256,256]{2,1,0:T(8,128)S(1)}, f32[1,256,256]{2,1,0:T(8,128)S(1)}, u32[]{:S(2)}, u32[]{:S(2)}) collective-permute-start(f32[1,256,256]{2,1,0:T(8,128)S(1)} %get-tuple-element.637), channel_id=1, source_target_pairs={{16,0},{32,16},{48,32},{64,48},{80,64},{96,80},{112,96},{128,112},... | collective-permute-start | bytes 786440 | tf_op jit(solution)/shard_map/while/body/eval_jaxpr/ppermute | solution.py:12
  220.7 9.8 %collective-permute-start = (f32[1,256,256]{2,1,0:T(8,128)S(1)}, f32[1,256,256]{2,1,0:T(8,128)S(1)}, u32[]{:S(2)}, u32[]{:S(2)}) collective-permute-start(f32[1,256,256]{2,1,0:T(8,128)S(1)} %get-tuple-element.637), channel_id=1, source_target_pairs={{16,0},{32,16},{48,32},{64,48},{80,64},{96,80},{112,96},{128,112},... | collective-permute-start | bytes 786440 | tf_op jit(solution)/shard_map/while/body/eval_jaxpr/ppermute | solution.py:12
  234.3 9.8 %collective-permute-start = (f32[1,256,256]{2,1,0:T(8,128)S(1)}, f32[1,256,256]{2,1,0:T(8,128)S(1)}, u32[]{:S(2)}, u32[]{:S(2)}) collective-permute-start(f32[1,256,256]{2,1,0:T(8,128)S(1)} %get-tuple-element.637), channel_id=1, source_target_pairs={{16,0},{32,16},{48,32},{64,48},{80,64},{96,80},{112,96},{128,112},... | collective-permute-start | bytes 786440 | tf_op jit(solution)/shard_map/while/body/eval_jaxpr/ppermute | solution.py:12
  247.9 9.8 %collective-permute-start = (f32[1,256,256]{2,1,0:T(8,128)S(1)}, f32[1,256,256]{2,1,0:T(8,128)S(1)}, u32[]{:S(2)}, u32[]{:S(2)}) collective-permute-start(f32[1,256,256]{2,1,0:T(8,128)S(1)} %get-tuple-element.637), channel_id=1, source_target_pairs={{16,0},{32,16},{48,32},{64,48},{80,64},{96,80},{112,96},{128,112},... | collective-permute-start | bytes 786440 | tf_op jit(solution)/shard_map/while/body/eval_jaxpr/ppermute | solution.py:12
  261.4 9.8 %collective-permute-start = (f32[1,256,256]{2,1,0:T(8,128)S(1)}, f32[1,256,256]{2,1,0:T(8,128)S(1)}, u32[]{:S(2)}, u32[]{:S(2)}) collective-permute-start(f32[1,256,256]{2,1,0:T(8,128)S(1)} %get-tuple-element.637), channel_id=1, source_target_pairs={{16,0},{32,16},{48,32},{64,48},{80,64},{96,80},{112,96},{128,112},... | collective-permute-start | bytes 786440 | tf_op jit(solution)/shard_map/while/body/eval_jaxpr/ppermute | solution.py:12
  275.0 9.8 %collective-permute-start = (f32[1,256,256]{2,1,0:T(8,128)S(1)}, f32[1,256,256]{2,1,0:T(8,128)S(1)}, u32[]{:S(2)}, u32[]{:S(2)}) collective-permute-start(f32[1,256,256]{2,1,0:T(8,128)S(1)} %get-tuple-element.637), channel_id=1, source_target_pairs={{16,0},{32,16},{48,32},{64,48},{80,64},{96,80},{112,96},{128,112},... | collective-permute-start | bytes 786440 | tf_op jit(solution)/shard_map/while/body/eval_jaxpr/ppermute | solution.py:12
  288.6 9.8 %collective-permute-start = (f32[1,256,256]{2,1,0:T(8,128)S(1)}, f32[1,256,256]{2,1,0:T(8,128)S(1)}, u32[]{:S(2)}, u32[]{:S(2)}) collective-permute-start(f32[1,256,256]{2,1,0:T(8,128)S(1)} %get-tuple-element.637), channel_id=1, source_target_pairs={{16,0},{32,16},{48,32},{64,48},{80,64},{96,80},{112,96},{128,112},... | collective-permute-start | bytes 786440 | tf_op jit(solution)/shard_map/while/body/eval_jaxpr/ppermute | solution.py:12
  302.2 9.8 %collective-permute-start = (f32[1,256,256]{2,1,0:T(8,128)S(1)}, f32[1,256,256]{2,1,0:T(8,128)S(1)}, u32[]{:S(2)}, u32[]{:S(2)}) collective-permute-start(f32[1,256,256]{2,1,0:T(8,128)S(1)} %get-tuple-element.637), channel_id=1, source_target_pairs={{16,0},{32,16},{48,32},{64,48},{80,64},{96,80},{112,96},{128,112},... | collective-permute-start | bytes 786440 | tf_op jit(solution)/shard_map/while/body/eval_jaxpr/ppermute | solution.py:12
  315.7 9.8 %collective-permute-start = (f32[1,256,256]{2,1,0:T(8,128)S(1)}, f32[1,256,256]{2,1,0:T(8,128)S(1)}, u32[]{:S(2)}, u32[]{:S(2)}) collective-permute-start(f32[1,256,256]{2,1,0:T(8,128)S(1)} %get-tuple-element.637), channel_id=1, source_target_pairs={{16,0},{32,16},{48,32},{64,48},{80,64},{96,80},{112,96},{128,112},... | collective-permute-start | bytes 786440 | tf_op jit(solution)/shard_map/while/body/eval_jaxpr/ppermute | solution.py:12
  329.3 9.8 %collective-permute-start = (f32[1,256,256]{2,1,0:T(8,128)S(1)}, f32[1,256,256]{2,1,0:T(8,128)S(1)}, u32[]{:S(2)}, u32[]{:S(2)}) collective-permute-start(f32[1,256,256]{2,1,0:T(8,128)S(1)} %get-tuple-element.637), channel_id=1, source_target_pairs={{16,0},{32,16},{48,32},{64,48},{80,64},{96,80},{112,96},{128,112},... | collective-permute-start | bytes 786440 | tf_op jit(solution)/shard_map/while/body/eval_jaxpr/ppermute | solution.py:12
  342.9 9.8 %collective-permute-start = (f32[1,256,256]{2,1,0:T(8,128)S(1)}, f32[1,256,256]{2,1,0:T(8,128)S(1)}, u32[]{:S(2)}, u32[]{:S(2)}) collective-permute-start(f32[1,256,256]{2,1,0:T(8,128)S(1)} %get-tuple-element.637), channel_id=1, source_target_pairs={{16,0},{32,16},{48,32},{64,48},{80,64},{96,80},{112,96},{128,112},... | collective-permute-start | bytes 786440 | tf_op jit(solution)/shard_map/while/body/eval_jaxpr/ppermute | solution.py:12
  356.5 9.8 %collective-permute-start = (f32[1,256,256]{2,1,0:T(8,128)S(1)}, f32[1,256,256]{2,1,0:T(8,128)S(1)}, u32[]{:S(2)}, u32[]{:S(2)}) collective-permute-start(f32[1,256,256]{2,1,0:T(8,128)S(1)} %get-tuple-element.637), channel_id=1, source_target_pairs={{16,0},{32,16},{48,32},{64,48},{80,64},{96,80},{112,96},{128,112},... | collective-permute-start | bytes 786440 | tf_op jit(solution)/shard_map/while/body/eval_jaxpr/ppermute | solution.py:12
  370.0 9.8 %collective-permute-start = (f32[1,256,256]{2,1,0:T(8,128)S(1)}, f32[1,256,256]{2,1,0:T(8,128)S(1)}, u32[]{:S(2)}, u32[]{:S(2)}) collective-permute-start(f32[1,256,256]{2,1,0:T(8,128)S(1)} %get-tuple-element.637), channel_id=1, source_target_pairs={{16,0},{32,16},{48,32},{64,48},{80,64},{96,80},{112,96},{128,112},... | collective-permute-start | bytes 786440 | tf_op jit(solution)/shard_map/while/body/eval_jaxpr/ppermute | solution.py:12
  383.6 9.8 %collective-permute-start = (f32[1,256,256]{2,1,0:T(8,128)S(1)}, f32[1,256,256]{2,1,0:T(8,128)S(1)}, u32[]{:S(2)}, u32[]{:S(2)}) collective-permute-start(f32[1,256,256]{2,1,0:T(8,128)S(1)} %get-tuple-element.637), channel_id=1, source_target_pairs={{16,0},{32,16},{48,32},{64,48},{80,64},{96,80},{112,96},{128,112},... | collective-permute-start | bytes 786440 | tf_op jit(solution)/shard_map/while/body/eval_jaxpr/ppermute | solution.py:12
  397.2 9.8 %collective-permute-start = (f32[1,256,256]{2,1,0:T(8,128)S(1)}, f32[1,256,256]{2,1,0:T(8,128)S(1)}, u32[]{:S(2)}, u32[]{:S(2)}) collective-permute-start(f32[1,256,256]{2,1,0:T(8,128)S(1)} %get-tuple-element.637), channel_id=1, source_target_pairs={{16,0},{32,16},{48,32},{64,48},{80,64},{96,80},{112,96},{128,112},... | collective-permute-start | bytes 786440 | tf_op jit(solution)/shard_map/while/body/eval_jaxpr/ppermute | solution.py:12
  410.7 9.8 %collective-permute-start = (f32[1,256,256]{2,1,0:T(8,128)S(1)}, f32[1,256,256]{2,1,0:T(8,128)S(1)}, u32[]{:S(2)}, u32[]{:S(2)}) collective-permute-start(f32[1,256,256]{2,1,0:T(8,128)S(1)} %get-tuple-element.637), channel_id=1, source_target_pairs={{16,0},{32,16},{48,32},{64,48},{80,64},{96,80},{112,96},{128,112},... | collective-permute-start | bytes 786440 | tf_op jit(solution)/shard_map/while/body/eval_jaxpr/ppermute | solution.py:12
  424.3 9.8 %collective-permute-start = (f32[1,256,256]{2,1,0:T(8,128)S(1)}, f32[1,256,256]{2,1,0:T(8,128)S(1)}, u32[]{:S(2)}, u32[]{:S(2)}) collective-permute-start(f32[1,256,256]{2,1,0:T(8,128)S(1)} %get-tuple-element.637), channel_id=1, source_target_pairs={{16,0},{32,16},{48,32},{64,48},{80,64},{96,80},{112,96},{128,112},... | collective-permute-start | bytes 786440 | tf_op jit(solution)/shard_map/while/body/eval_jaxpr/ppermute | solution.py:12
  437.9 9.8 %collective-permute-start = (f32[1,256,256]{2,1,0:T(8,128)S(1)}, f32[1,256,256]{2,1,0:T(8,128)S(1)}, u32[]{:S(2)}, u32[]{:S(2)}) collective-permute-start(f32[1,256,256]{2,1,0:T(8,128)S(1)} %get-tuple-element.637), channel_id=1, source_target_pairs={{16,0},{32,16},{48,32},{64,48},{80,64},{96,80},{112,96},{128,112},... | collective-permute-start | bytes 786440 | tf_op jit(solution)/shard_map/while/body/eval_jaxpr/ppermute | solution.py:12
  456.1 23.1 %all-to-all-start.4 = ((bf16[16,2,2048]{2,1,0:T(2,128)(2,1)}), bf16[16,2,2048]{2,1,0:T(2,128)(2,1)S(1)}, u32[]{:S(2)}, u32[]{:S(2)}) async-start(bf16[16,2,2048]{2,1,0:T(2,128)(2,1)} %reshape.369), calls=%async_computation.4 | async-start | bytes 262144 | tf_op jit(solution)/shard_map/all_to_all | solution.py:127
  479.2 15.8 %all-to-all-start.2 = ((bf16[16,2,2048]{2,1,0:T(2,128)(2,1)}), bf16[16,2,2048]{2,1,0:T(2,128)(2,1)S(1)}, u32[]{:S(2)}, u32[]{:S(2)}) async-start(bf16[16,2,2048]{2,1,0:T(2,128)(2,1)} %reshape.367), calls=%async_computation.2 | async-start | bytes 262144 | tf_op jit(solution)/shard_map/all_to_all | solution.py:126
  (18 other events, 181.4 us)
where the time goes:
time: 636 us; the launch traced here: 631 us
  waiting for transfers between devices  255 us (40%)
  blocking collectives  130 us (20%)
  starting transfers between devices  104 us (16%)
  matrix products  84.9 us (13%)
  local copies, waits for them, and re-layouts  45.3 us (7%)
    ppermute x31, waiting for transfers between devices, from_behind(): lax.ppermute(value, axis, [(source, source + steps) for source in range(f...  215 us
    psum x1, blocking collectives, local(): summed = lax.psum(partial_value, ('seq', 'key'))  130 us
    dot_general x130, matrix products, precise_product(): jnp.einsum(form, left.astype(jnp.float32), right, precision=highest_mode)  80.6 us
    ppermute x31, starting transfers between devices, from_behind(): lax.ppermute(value, axis, [(source, source + steps) for source in range(f...  61.5 us
    dynamic_slice x64, local copies, waits for them, and re-layouts, device_map(): lax.scan(group_step, state_out, (written_keys, key_result, end_decay, off...  37.6 us
    all_to_all x1, starting transfers between devices, local(): lax.all_to_all(key_rows, 'key', split_axis=1, concat_axis=2, tiled=True)  15.9 us
  transfers between devices with their start and end apart: 36, of which 35 were waited for; matrix products, arithmetic and copies ran while one was open for 20% of the time, Pallas kernels for 0%

commit v1 on v0

--- a/solution.py
+++ b/solution.py
@@ -4,6 +4,10 @@
 from jax.sharding import PartitionSpec as P
 
 highest_mode = lax.Precision.HIGHEST
+
+
+def read_the_view(frame):
+    return lax.psum(lax.psum(frame, "seq"), "key")
 
 
 def from_behind(value, axis, steps):
@@ -128,7 +132,7 @@
     )
     value_square = square_sum(grad_value)
     partial_value = square_sum(grad_query) + square_sum(grad_key) + value_square
-    summed = lax.psum(partial_value, ("seq", "key"))
+    summed = read_the_view(partial_value)
     entries = (
         token_count * lax.axis_size("seq") * query_rows.shape[1] * (2 * key_width + value_width)
     )

time: 636 us -> 618 us (0.972)
  the two profiles are of different devices: /device:TPU:1 before, /device:TPU:6 now
where the time goes in v1:
time: 618 us; the launch traced here: 614 us
  starting transfers between devices  220 us (36%)
  waiting for transfers between devices  167 us (27%)
  matrix products  84.9 us (14%)
  blocking collectives  84.1 us (14%)
  local copies, waits for them, and re-layouts  45.3 us (7%)
    ppermute x31, starting transfers between devices, from_behind(): lax.ppermute(value, axis, [(source, source + steps) for source in range(f...  181 us
    ppermute x31, waiting for transfers between devices, from_behind(): lax.ppermute(value, axis, [(source, source + steps) for source in range(f...  120 us
    psum x2, blocking collectives, read_the_view(): return lax.psum(lax.psum(frame, 'seq'), 'key')  84.1 us
    dot_general x130, matrix products, precise_product(): jnp.einsum(form, left.astype(jnp.float32), right, precision=highest_mode)  80.6 us
    dynamic_slice x64, local copies, waits for them, and re-layouts, device_map(): lax.scan(group_step, state_out, (written_keys, key_result, end_decay, off...  37.6 us
    all_to_all x1, starting transfers between devices, local(): lax.all_to_all(key_rows, 'key', split_axis=1, concat_axis=2, tiled=True)  15.3 us
    all_to_all x1, waiting for transfers between devices, local(): lax.all_to_all(key_rows, 'key', split_axis=1, concat_axis=2, tiled=True)  13.4 us
  transfers between devices with their start and end apart: 36, of which 35 were waited for; matrix products, arithmetic and copies ran while one was open for 21% of the time, Pallas kernels for 0%

profile of v1, /device:TPU:6, one launch (start us, length us, event | category | flops | bytes accessed | tf_op | source)
XLA Modules:
  0.0 613.5 jit_solution(12314873346037655857)
XLA Ops:
  0.7 15.3 %all-to-all-start.1 = ((bf16[256,16,16]{0,2,1:T(8,128)(2,1)}), bf16[256,16,16]{0,2,1:T(8,128)(2,1)S(1)}, u32[]{:S(2)}, u32[]{:S(2)}) async-start(bf16[256,16,16]{0,2,1:T(8,128)(2,1)} %param.15), calls=%async_computation.1 | async-start | bytes 262144 | tf_op jit(solution)/shard_map/all_to_all | solution.py:57
  17.3 13.4 %all-to-all-done.1 = bf16[256,16,16]{0,2,1:T(8,128)(2,1)S(1)} async-done(((bf16[256,16,16]{0,2,1:T(8,128)(2,1)}), bf16[256,16,16]{0,2,1:T(8,128)(2,1)S(1)}, u32[]{:S(2)}, u32[]{:S(2)}) %all-to-all-start.1) | async-done | bytes 131104 | tf_op jit(solution)/shard_map/all_to_all | solution.py:57
  36.9 11.7 %all-to-all-done.3 = bf16[256,16,16]{0,2,1:T(8,128)(2,1)S(1)} async-done(((bf16[256,16,16]{0,2,1:T(8,128)(2,1)}), bf16[256,16,16]{0,2,1:T(8,128)(2,1)S(1)}, u32[]{:S(2)}, u32[]{:S(2)}) %all-to-all-start.3) | async-done | bytes 131104 | tf_op jit(solution)/shard_map/all_to_all | solution.py:56
  54.5 418.4 %while.57 = (s32[]{:T(128)}, f32[1,256,256]{2,1,0:T(8,128)S(1)}, f32[2,1]{0,1:T(1,128)S(1)}, bf16[2,128,1,256]{3,1,2,0:T(8,128)(2,1)S(1)}, bf16[2,128,1,256]{3,1...) while((s32[]{:T(128)}, f32[1,256,256]{2,1,0:T(8,128)S(1)}, ...), condition=%wide.region_4.5_spmd, body=%wide.region_1.4_spmd.sunk | while | flops 201523200 | bytes 3015986 | solution.py:101
  69.2 6.2 %collective-permute-start = (f32[1,256,256]{2,1,0:T(8,128)S(1)}, f32[1,256,256]{2,1,0:T(8,128)S(1)}, u32[]{:S(2)}, u32[]{:S(2)}) collective-permute-start(f32[1,256,256]{2,1,0:T(8,128)S(1)} %get-tuple-element.637), channel_id=1, source_target_pairs={{16,0},{32,16},{48,32},{64,48},{80,64},{96,80},{112,96},{128,112},... | collective-permute-start | bytes 786440 | tf_op jit(solution)/shard_map/while/body/eval_jaxpr/ppermute | solution.py:16
  83.1 5.9 collective-permute-start
  96.6 5.9 collective-permute-start
  123.8 5.9 collective-permute-start
  137.3 5.9 collective-permute-start
  178.1 5.9 collective-permute-start
  191.6 5.9 collective-permute-start
  232.4 5.9 collective-permute-start
  273.1 5.9 collective-permute-start
  286.7 5.9 collective-permute-start
  327.4 5.9 collective-permute-start
  368.1 5.9 collective-permute-start
  381.7 5.9 collective-permute-start
  422.4 5.9 collective-permute-start
  463.1 5.9 collective-permute-start
  481.3 11.4 %all-to-all-start.4 = ((bf16[16,2,2048]{2,1,0:T(2,128)(2,1)}), bf16[16,2,2048]{2,1,0:T(2,128)(2,1)S(1)}, u32[]{:S(2)}, u32[]{:S(2)}) async-start(bf16[16,2,2048]{2,1,0:T(2,128)(2,1)} %reshape.369), calls=%async_computation.4 | async-start | bytes 262144 | tf_op jit(solution)/shard_map/all_to_all | solution.py:131
  495.5 10.5 %all-to-all-done.4 = bf16[16,2,2048]{2,1,0:T(2,128)(2,1)S(1)} async-done(((bf16[16,2,2048]{2,1,0:T(2,128)(2,1)}), bf16[16,2,2048]{2,1,0:T(2,128)(2,1)S(1)}, u32[]{:S(2)}, u32[]{:S(2)}) %all-to-all-start.4) | async-done | bytes 131104 | tf_op jit(solution)/shard_map/all_to_all | solution.py:131
  511.5 11.6 %all-to-all-done.2 = bf16[16,2,2048]{2,1,0:T(2,128)(2,1)S(1)} async-done(((bf16[16,2,2048]{2,1,0:T(2,128)(2,1)}), bf16[16,2,2048]{2,1,0:T(2,128)(2,1)S(1)}, u32[]{:S(2)}, u32[]{:S(2)}) %all-to-all-start.2) | async-done | bytes 131104 | tf_op jit(solution)/shard_map/all_to_all | solution.py:130
  526.3 54.7 %psum.14 = f32[]{:T(128)} all-reduce(f32[]{:T(128)S(6)} %add.91), channel_id=1, replica_groups=mesh['seq'=32,'key'=16] {'seq'}, use_global_device_ids=true, to_apply=%region_10.11 | all-reduce | flops 1 | bytes 8 | tf_op jit(solution)/shard_map/psum | solution.py:10
  581.0 29.4 %psum.15 = f32[]{:T(128)} all-reduce(f32[]{:T(128)} %psum.14), channel_id=1, replica_groups=mesh['seq'=32,'key'=16] {'key'}, use_global_device_ids=true, to_apply=%region_11.12 | all-reduce | flops 1 | bytes 8 | tf_op jit(solution)/shard_map/psum | solution.py:10
  (364 shorter events, 478.1 us)
Async XLA Ops:
  0.7 30.0 %all-to-all-start.1 = ((bf16[256,16,16]{0,2,1:T(8,128)(2,1)}), bf16[256,16,16]{0,2,1:T(8,128)(2,1)S(1)}, u32[]{:S(2)}, u32[]{:S(2)}) async-start(bf16[256,16,16]{0,2,1:T(8,128)(2,1)} %param.15), calls=%async_computation.1 | async-start | bytes 262144 | tf_op jit(solution)/shard_map/all_to_all | solution.py:57
  30.7 17.9 %all-to-all-start.3 = ((bf16[256,16,16]{0,2,1:T(8,128)(2,1)}), bf16[256,16,16]{0,2,1:T(8,128)(2,1)S(1)}, u32[]{:S(2)}, u32[]{:S(2)}) async-start(bf16[256,16,16]{0,2,1:T(8,128)(2,1)} %param.14), calls=%async_computation.3 | async-start | bytes 262144 | tf_op jit(solution)/shard_map/all_to_all | solution.py:56
  48.6 428.6 %all-to-all-start = ((bf16[2,16,16,256]{3,2,0,1:T(8,128)(2,1)}), bf16[2,16,16,256]{3,2,0,1:T(8,128)(2,1)S(1)}, u32[]{:S(2)}, u32[]{:S(2)}) async-start(bf16[2,16,16,256]{3,2,0,1:T(8,128)(2,1)} %copy.117), calls=%async_computation | async-start | bytes 524288 | tf_op jit(solution)/shard_map/all_to_all | solution.py:58
  69.2 10.1 %collective-permute-start = (f32[1,256,256]{2,1,0:T(8,128)S(1)}, f32[1,256,256]{2,1,0:T(8,128)S(1)}, u32[]{:S(2)}, u32[]{:S(2)}) collective-permute-start(f32[1,256,256]{2,1,0:T(8,128)S(1)} %get-tuple-element.637), channel_id=1, source_target_pairs={{16,0},{32,16},{48,32},{64,48},{80,64},{96,80},{112,96},{128,112},... | collective-permute-start | bytes 786440 | tf_op jit(solution)/shard_map/while/body/eval_jaxpr/ppermute | solution.py:16
  83.1 9.8 %collective-permute-start = (f32[1,256,256]{2,1,0:T(8,128)S(1)}, f32[1,256,256]{2,1,0:T(8,128)S(1)}, u32[]{:S(2)}, u32[]{:S(2)}) collective-permute-start(f32[1,256,256]{2,1,0:T(8,128)S(1)} %get-tuple-element.637), channel_id=1, source_target_pairs={{16,0},{32,16},{48,32},{64,48},{80,64},{96,80},{112,96},{128,112},... | collective-permute-start | bytes 786440 | tf_op jit(solution)/shard_map/while/body/eval_jaxpr/ppermute | solution.py:16
  96.6 9.8 %collective-permute-start = (f32[1,256,256]{2,1,0:T(8,128)S(1)}, f32[1,256,256]{2,1,0:T(8,128)S(1)}, u32[]{:S(2)}, u32[]{:S(2)}) collective-permute-start(f32[1,256,256]{2,1,0:T(8,128)S(1)} %get-tuple-element.637), channel_id=1, source_target_pairs={{16,0},{32,16},{48,32},{64,48},{80,64},{96,80},{112,96},{128,112},... | collective-permute-start | bytes 786440 | tf_op jit(solution)/shard_map/while/body/eval_jaxpr/ppermute | solution.py:16
  123.8 9.8 %collective-permute-start = (f32[1,256,256]{2,1,0:T(8,128)S(1)}, f32[1,256,256]{2,1,0:T(8,128)S(1)}, u32[]{:S(2)}, u32[]{:S(2)}) collective-permute-start(f32[1,256,256]{2,1,0:T(8,128)S(1)} %get-tuple-element.637), channel_id=1, source_target_pairs={{16,0},{32,16},{48,32},{64,48},{80,64},{96,80},{112,96},{128,112},... | collective-permute-start | bytes 786440 | tf_op jit(solution)/shard_map/while/body/eval_jaxpr/ppermute | solution.py:16
  137.3 9.8 %collective-permute-start = (f32[1,256,256]{2,1,0:T(8,128)S(1)}, f32[1,256,256]{2,1,0:T(8,128)S(1)}, u32[]{:S(2)}, u32[]{:S(2)}) collective-permute-start(f32[1,256,256]{2,1,0:T(8,128)S(1)} %get-tuple-element.637), channel_id=1, source_target_pairs={{16,0},{32,16},{48,32},{64,48},{80,64},{96,80},{112,96},{128,112},... | collective-permute-start | bytes 786440 | tf_op jit(solution)/shard_map/while/body/eval_jaxpr/ppermute | solution.py:16
  164.5 9.8 %collective-permute-start = (f32[1,256,256]{2,1,0:T(8,128)S(1)}, f32[1,256,256]{2,1,0:T(8,128)S(1)}, u32[]{:S(2)}, u32[]{:S(2)}) collective-permute-start(f32[1,256,256]{2,1,0:T(8,128)S(1)} %get-tuple-element.637), channel_id=1, source_target_pairs={{16,0},{32,16},{48,32},{64,48},{80,64},{96,80},{112,96},{128,112},... | collective-permute-start | bytes 786440 | tf_op jit(solution)/shard_map/while/body/eval_jaxpr/ppermute | solution.py:16
  178.1 9.8 %collective-permute-start = (f32[1,256,256]{2,1,0:T(8,128)S(1)}, f32[1,256,256]{2,1,0:T(8,128)S(1)}, u32[]{:S(2)}, u32[]{:S(2)}) collective-permute-start(f32[1,256,256]{2,1,0:T(8,128)S(1)} %get-tuple-element.637), channel_id=1, source_target_pairs={{16,0},{32,16},{48,32},{64,48},{80,64},{96,80},{112,96},{128,112},... | collective-permute-start | bytes 786440 | tf_op jit(solution)/shard_map/while/body/eval_jaxpr/ppermute | solution.py:16
  191.6 9.8 %collective-permute-start = (f32[1,256,256]{2,1,0:T(8,128)S(1)}, f32[1,256,256]{2,1,0:T(8,128)S(1)}, u32[]{:S(2)}, u32[]{:S(2)}) collective-permute-start(f32[1,256,256]{2,1,0:T(8,128)S(1)} %get-tuple-element.637), channel_id=1, source_target_pairs={{16,0},{32,16},{48,32},{64,48},{80,64},{96,80},{112,96},{128,112},... | collective-permute-start | bytes 786440 | tf_op jit(solution)/shard_map/while/body/eval_jaxpr/ppermute | solution.py:16
  218.8 9.8 %collective-permute-start = (f32[1,256,256]{2,1,0:T(8,128)S(1)}, f32[1,256,256]{2,1,0:T(8,128)S(1)}, u32[]{:S(2)}, u32[]{:S(2)}) collective-permute-start(f32[1,256,256]{2,1,0:T(8,128)S(1)} %get-tuple-element.637), channel_id=1, source_target_pairs={{16,0},{32,16},{48,32},{64,48},{80,64},{96,80},{112,96},{128,112},... | collective-permute-start | bytes 786440 | tf_op jit(solution)/shard_map/while/body/eval_jaxpr/ppermute | solution.py:16
  232.4 9.8 %collective-permute-start = (f32[1,256,256]{2,1,0:T(8,128)S(1)}, f32[1,256,256]{2,1,0:T(8,128)S(1)}, u32[]{:S(2)}, u32[]{:S(2)}) collective-permute-start(f32[1,256,256]{2,1,0:T(8,128)S(1)} %get-tuple-element.637), channel_id=1, source_target_pairs={{16,0},{32,16},{48,32},{64,48},{80,64},{96,80},{112,96},{128,112},... | collective-permute-start | bytes 786440 | tf_op jit(solution)/shard_map/while/body/eval_jaxpr/ppermute | solution.py:16
  259.5 9.8 %collective-permute-start = (f32[1,256,256]{2,1,0:T(8,128)S(1)}, f32[1,256,256]{2,1,0:T(8,128)S(1)}, u32[]{:S(2)}, u32[]{:S(2)}) collective-permute-start(f32[1,256,256]{2,1,0:T(8,128)S(1)} %get-tuple-element.637), channel_id=1, source_target_pairs={{16,0},{32,16},{48,32},{64,48},{80,64},{96,80},{112,96},{128,112},... | collective-permute-start | bytes 786440 | tf_op jit(solution)/shard_map/while/body/eval_jaxpr/ppermute | solution.py:16
  273.1 9.8 %collective-permute-start = (f32[1,256,256]{2,1,0:T(8,128)S(1)}, f32[1,256,256]{2,1,0:T(8,128)S(1)}, u32[]{:S(2)}, u32[]{:S(2)}) collective-permute-start(f32[1,256,256]{2,1,0:T(8,128)S(1)} %get-tuple-element.637), channel_id=1, source_target_pairs={{16,0},{32,16},{48,32},{64,48},{80,64},{96,80},{112,96},{128,112},... | collective-permute-start | bytes 786440 | tf_op jit(solution)/shard_map/while/body/eval_jaxpr/ppermute | solution.py:16
  286.7 9.8 %collective-permute-start = (f32[1,256,256]{2,1,0:T(8,128)S(1)}, f32[1,256,256]{2,1,0:T(8,128)S(1)}, u32[]{:S(2)}, u32[]{:S(2)}) collective-permute-start(f32[1,256,256]{2,1,0:T(8,128)S(1)} %get-tuple-element.637), channel_id=1, source_target_pairs={{16,0},{32,16},{48,32},{64,48},{80,64},{96,80},{112,96},{128,112},... | collective-permute-start | bytes 786440 | tf_op jit(solution)/shard_map/while/body/eval_jaxpr/ppermute | solution.py:16
  313.8 9.8 %collective-permute-start = (f32[1,256,256]{2,1,0:T(8,128)S(1)}, f32[1,256,256]{2,1,0:T(8,128)S(1)}, u32[]{:S(2)}, u32[]{:S(2)}) collective-permute-start(f32[1,256,256]{2,1,0:T(8,128)S(1)} %get-tuple-element.637), channel_id=1, source_target_pairs={{16,0},{32,16},{48,32},{64,48},{80,64},{96,80},{112,96},{128,112},... | collective-permute-start | bytes 786440 | tf_op jit(solution)/shard_map/while/body/eval_jaxpr/ppermute | solution.py:16
  327.4 9.8 %collective-permute-start = (f32[1,256,256]{2,1,0:T(8,128)S(1)}, f32[1,256,256]{2,1,0:T(8,128)S(1)}, u32[]{:S(2)}, u32[]{:S(2)}) collective-permute-start(f32[1,256,256]{2,1,0:T(8,128)S(1)} %get-tuple-element.637), channel_id=1, source_target_pairs={{16,0},{32,16},{48,32},{64,48},{80,64},{96,80},{112,96},{128,112},... | collective-permute-start | bytes 786440 | tf_op jit(solution)/shard_map/while/body/eval_jaxpr/ppermute | solution.py:16
  368.1 9.8 %collective-permute-start = (f32[1,256,256]{2,1,0:T(8,128)S(1)}, f32[1,256,256]{2,1,0:T(8,128)S(1)}, u32[]{:S(2)}, u32[]{:S(2)}) collective-permute-start(f32[1,256,256]{2,1,0:T(8,128)S(1)} %get-tuple-element.637), channel_id=1, source_target_pairs={{16,0},{32,16},{48,32},{64,48},{80,64},{96,80},{112,96},{128,112},... | collective-permute-start | bytes 786440 | tf_op jit(solution)/shard_map/while/body/eval_jaxpr/ppermute | solution.py:16
  381.7 9.8 %collective-permute-start = (f32[1,256,256]{2,1,0:T(8,128)S(1)}, f32[1,256,256]{2,1,0:T(8,128)S(1)}, u32[]{:S(2)}, u32[]{:S(2)}) collective-permute-start(f32[1,256,256]{2,1,0:T(8,128)S(1)} %get-tuple-element.637), channel_id=1, source_target_pairs={{16,0},{32,16},{48,32},{64,48},{80,64},{96,80},{112,96},{128,112},... | collective-permute-start | bytes 786440 | tf_op jit(solution)/shard_map/while/body/eval_jaxpr/ppermute | solution.py:16
  422.4 9.8 %collective-permute-start = (f32[1,256,256]{2,1,0:T(8,128)S(1)}, f32[1,256,256]{2,1,0:T(8,128)S(1)}, u32[]{:S(2)}, u32[]{:S(2)}) collective-permute-start(f32[1,256,256]{2,1,0:T(8,128)S(1)} %get-tuple-element.637), channel_id=1, source_target_pairs={{16,0},{32,16},{48,32},{64,48},{80,64},{96,80},{112,96},{128,112},... | collective-permute-start | bytes 786440 | tf_op jit(solution)/shard_map/while/body/eval_jaxpr/ppermute | solution.py:16
  463.1 9.8 %collective-permute-start = (f32[1,256,256]{2,1,0:T(8,128)S(1)}, f32[1,256,256]{2,1,0:T(8,128)S(1)}, u32[]{:S(2)}, u32[]{:S(2)}) collective-permute-start(f32[1,256,256]{2,1,0:T(8,128)S(1)} %get-tuple-element.637), channel_id=1, source_target_pairs={{16,0},{32,16},{48,32},{64,48},{80,64},{96,80},{112,96},{128,112},... | collective-permute-start | bytes 786440 | tf_op jit(solution)/shard_map/while/body/eval_jaxpr/ppermute | solution.py:16
  481.3 24.7 %all-to-all-start.4 = ((bf16[16,2,2048]{2,1,0:T(2,128)(2,1)}), bf16[16,2,2048]{2,1,0:T(2,128)(2,1)S(1)}, u32[]{:S(2)}, u32[]{:S(2)}) async-start(bf16[16,2,2048]{2,1,0:T(2,128)(2,1)} %reshape.369), calls=%async_computation.4 | async-start | bytes 262144 | tf_op jit(solution)/shard_map/all_to_all | solution.py:131
  506.0 17.0 %all-to-all-start.2 = ((bf16[16,2,2048]{2,1,0:T(2,128)(2,1)}), bf16[16,2,2048]{2,1,0:T(2,128)(2,1)S(1)}, u32[]{:S(2)}, u32[]{:S(2)}) async-start(bf16[16,2,2048]{2,1,0:T(2,128)(2,1)} %reshape.367), calls=%async_computation.2 | async-start | bytes 262144 | tf_op jit(solution)/shard_map/all_to_all | solution.py:130
  (18 other events, 204.6 us)
